TPU v7x, 32 devices: a whole 2x2x4 slice. The times are simulated.
32 devices in a mesh: groups: 2 (over x), docs: 8 (over z, y), layers: 2 (over core).
Axes of the slice: x: 2, y: 2, z: 4, core: 2. Of those that a mesh axis runs over, the one named last changes fastest.
Arguments:
- doc_grads: bfloat16 [12288, 4, 4096], P(('groups', 'docs'), 'layers'), parts along dimension 0, may hold values from -6 to 6
- query_grads: bfloat16 [512, 4, 4096], P(('groups', 'docs'), 'layers'), parts along dimension 0, may hold values from -0.046875 to 0.046875
- doc_lengths: int32 [12288], P(('groups', 'docs')), parts along dimension 0, may hold values from 1 to 16
Outputs:
- scores: float32 [12288, 256], P(('groups', 'docs'), 'layers'), parts along dimension 0
There are 2 independent parts, one for each index of `groups`. A program takes and returns all parts, laid end to end along the dimension named above; each array names one. Nothing has to cross between parts.
All inputs are finite; a program needn't handle non-finite values.
Results may differ from a plain program's by a relative error of at most 0.0003.
Values may be sent and summed in bfloat16 or wider, within the bound.
A program may use at most 64 MiB of HBM per device.

v0:
```python
import jax
import jax.numpy as jnp
from jax import lax
from jax.sharding import PartitionSpec as P


def on_device(doc_grads, query_grads, doc_lengths):
    partial_value = jnp.einsum(
        "dlp,qlp->dq",
        doc_grads,
        lax.all_gather(query_grads, "docs", axis=0, tiled=True),
        preferred_element_type=jnp.float32,
    )
    summed = lax.psum_scatter(partial_value, "layers", scatter_dimension=1, tiled=True)
    return summed / doc_lengths.astype(jnp.float32)[:, None]


def solution(mesh):
    in_specs = (
        P(("groups", "docs"), "layers", None),
        P(("groups", "docs"), "layers", None),
        P(("groups", "docs")),
    )
    out_specs = P(("groups", "docs"), "layers")
    return jax.shard_map(
        on_device, mesh=mesh, in_specs=in_specs, out_specs=out_specs, check_vma=False
    )
```

profile of v0, /device:TPU:0, one launch (start us, length us, event | category | flops | bytes accessed | tf_op | source)
XLA Modules:
  0.0 115.0 jit_solution(2527866026285071045)
XLA Ops:
  6.5 0.0 all-gather.2.cloned.1.call-start
  6.5 2.2 %copy.4 = bf16[32,2,4096]{2,0,1:T(8,128)(2,1)} copy(bf16[32,2,4096]{2,1,0:T(2,128)(2,1)} %param.4) | data formatting | bytes 1048576 | tf_op args[1]
  8.7 0.0 all-gather.2.cloned.1.call-update
  8.7 0.0 copy-start
  8.7 0.0 reduce-scatter.2.cloned.1.call-start
  8.8 76.9 %all-gather.2.cloned.1.call-done = bf16[256,2,4096]{2,0,1:T(8,128)(2,1)} async-done(((bf16[32,2,4096]{2,0,1:T(8,128)(2,1)}), bf16[256,2,4096]{2,0,1:T(8,128)(2,1)}) %all-gather.2.cloned.1.call-update) | async-done | bytes 4194320 | tf_op jit(solution)/shard_map/all_gather | solution.py:11
  85.7 13.9 %fusion.2 = f32[768,256]{1,0:T(8,128)} fusion(bf16[256,2,4096]{2,0,1:T(8,128)(2,1)} %all-gather.2.cloned.1.call-done, bf16[768,2,4096]{2,1,0:T(2,128)(2,1)} %param.3), kind=kOutput, calls=%fused_computation.2 | convolution fusion | flops 3221225472 | bytes 17563648 | tf_op jit(solution)/shard_map/dlp,qlp->dq/dot_general | solution.py:8
  99.5 0.0 reduce-scatter.2.cloned.1.call-update
  99.5 0.0 copy-done
  99.6 6.6 %reduce-scatter.2.cloned.1.call-done = f32[768,128]{1,0:T(8,128)} async-done(((f32[768,256]{1,0:T(8,128)}), f32[768,128]{1,0:T(8,128)}) %reduce-scatter.2.cloned.1.call-update) | async-done | bytes 393232 | tf_op jit(solution)/shard_map/reduce_scatter | solution.py:14
  106.2 1.9 %broadcast_divide_fusion = f32[768,128]{1,0:T(8,128)} fusion(f32[768,128]{1,0:T(8,128)} %reduce-scatter.2.cloned.1.call-done, f32[768]{0:T(1024)S(1)} %convert_element_type.3), kind=kLoop, calls=%fused_computation.3 | loop fusion | flops 98304 | bytes 789504 | tf_op jit(solution)/shard_map/div | solution.py:15
  (1 shorter events, 0.0 us)
Async XLA Ops:
  6.5 79.1 %all-gather.2.cloned.1.call-start = ((), (), s32[]{:S(2)}) async-start(), calls=%async_computation.1 | async-start | bytes 4718592 | tf_op jit(solution)/shard_map/all_gather | solution.py:11
  8.7 90.8 %copy-start = (s32[768]{0:T(1024)S(1)}, s32[768]{0:T(1024)}, u32[]{:S(2)}) copy-start(s32[768]{0:T(1024)} %param.5) | copy-start | bytes 9220
  8.7 97.5 %reduce-scatter.2.cloned.1.call-start = ((), (), s32[]{:S(2)}) async-start(), calls=%async_computation.2 | async-start | bytes 1179648 | tf_op jit(solution)/shard_map/reduce_scatter | solution.py:14
Sparse Core Ops, SparseCore 0:
  9.5 76.0 all-gather.1
  99.7 6.4 reduce-scatter.1
where the time goes:
time: 115 us
  waiting for transfers between devices  83.5 us (73%)
  matrix products  13.9 us (12%)
  between operations  13.4 us (12%)
  local copies, waits for them, and re-layouts  2.16 us (2%)
  other arithmetic  1.92 us (2%)
    all_gather x1, waiting for transfers between devices, on_device(): lax.all_gather(query_grads, 'docs', axis=0, tiled=True)  76.9 us
    dot_general x1, matrix products, on_device(): jnp.einsum('dlp,qlp->dq', doc_grads, lax.all_gather(query_grads, 'docs',...  13.9 us
    reduce_scatter x1, waiting for transfers between devices, on_device(): lax.psum_scatter(partial_value, 'layers', scatter_dimension=1, tiled=True)  6.64 us
  transfers between devices with their start and end apart: 2, of which 2 were waited for; matrix products, arithmetic and copies ran while one was open for 0% of the time, Pallas kernels for 0%

commit v1 on v0

--- a/solution.py
+++ b/solution.py
@@ -1,10 +1,254 @@
+import functools
+
 import jax
 import jax.numpy as jnp
 from jax import lax
+from jax.experimental import pallas as pl
+from jax.experimental.pallas import tpu as pltpu
 from jax.sharding import PartitionSpec as P
 
-
-def on_device(doc_grads, query_grads, doc_lengths):
+LINE = 4
+LAST = 640
+STEP = 512
+LAG = 5
+
+
+def pieces_of(depth):
+    cuts, at = [], 0
+    while at < depth - LAST:
+        size = min(STEP, depth - LAST - at)
+        cuts.append((at, size))
+        at += size
+    return cuts + [(at, depth - at)]
+
+
+def kernel(cuts, docs_ref, q_ref, len_ref, out_ref, docs, own_q, held, acc, other, lengths,
+           doc_sem, q_sem, send_sem, recv_sem, x_send, x_recv):
+    me = lax.axis_index("docs")
+    core = lax.axis_index("layers")
+    z, y = me // 2, me % 2
+    across = z * 2 + (1 - y)
+    rows = q_ref.shape[0]
+    last = len(cuts) - 1
+    n_docs = docs.shape[0]
+    half = out_ref.shape[1]
+
+    def q_copy(c):
+        at, size = cuts[c]
+        cols = pl.ds(at, size)
+        return pltpu.make_async_copy(q_ref.at[:, :, cols], own_q.at[:, :, cols], q_sem.at[c])
+
+    def doc_copy(c):
+        at, size = cuts[c]
+        cols = pl.ds(at, size)
+        return pltpu.make_async_copy(docs_ref.at[:, :, cols], docs.at[:, :, cols], doc_sem.at[c])
+
+    first = [0, last] + list(range(1, last))
+    for c in first:
+        q_copy(c).start()
+    for c in range(last + 1):
+        doc_copy(c).start()
+
+    barrier = pltpu.get_barrier_semaphore()
+
+    def greet(target):
+        pl.semaphore_signal(barrier, inc=1, device_id=target, device_id_type=pl.DeviceIdType.MESH)
+
+    greet({"docs": across})
+    greet({"layers": 1 - core})
+
+    @pl.when(z < LINE - 1)
+    def _():
+        greet({"docs": me + 2})
+
+    @pl.when(z > 0)
+    def _():
+        greet({"docs": me - 2})
+
+    def take_own(c):
+        at, size = cuts[c]
+        q_copy(c).wait()
+        mine = pl.ds(pl.multiple_of(me * rows, rows), rows)
+        for layer in range(2):
+            held[layer, mine, pl.ds(at, size)] = own_q[:, layer, pl.ds(at, size)]
+
+    take_own(0)
+    take_own(last)
+
+    pl.semaphore_wait(barrier, 2 + (z + LINE - 1) // LINE + (2 * LINE - 2 - z) // LINE)
+
+    def copy(c, src, way):
+        at, size = cuts[c]
+        block = held.at[:, pl.ds(pl.multiple_of(src * rows, rows), rows), pl.ds(at, size)]
+        return pltpu.make_async_remote_copy(
+            src_ref=block,
+            dst_ref=block,
+            send_sem=send_sem.at[way, c, src],
+            recv_sem=recv_sem.at[c, src],
+            device_id={"docs": (me + 2, me - 2, across)[way]},
+            device_id_type=pl.DeviceIdType.MESH,
+        )
+
+    def arrived(c, src, start):
+        if start:
+            copy(c, src, 2).wait_recv()
+
+    def send(c, src, way, start):
+        def act():
+            if start:
+                copy(c, src, way).start()
+            else:
+                copy(c, src, way).wait_send()
+
+        if way == 0:
+            pl.when(z < LINE - 1)(act)
+        elif way == 1:
+            pl.when(z > 0)(act)
+        else:
+            act()
+
+    def stage(c, hops, start=True):
+        if hops == 0:
+            send(c, me, 0, start)
+            send(c, me, 1, start)
+            if c == last:
+                arrived(c, across, start)
+                send(c, across, 0, start)
+                send(c, across, 1, start)
+            else:
+                send(c, me, 2, start)
+            return
+        for lane in (y,) if c < last else (y, 1 - y):
+
+            @pl.when(z >= hops)
+            def _():
+                src = (z - hops) * 2 + lane
+                arrived(c, src, start)
+                send(c, src, 0, start)
+                if c < last:
+                    send(c, src, 2, start)
+
+            @pl.when(z + hops < LINE)
+            def _():
+                src = (z + hops) * 2 + lane
+                arrived(c, src, start)
+                send(c, src, 1, start)
+                if c < last:
+                    send(c, src, 2, start)
+
+    def add(c, at_row, n_rows, first_one):
+        at, size = cuts[c]
+        these = pl.ds(at_row, n_rows)
+        cols = pl.ds(at, size)
+        total = None
+        for layer in range(2):
+            term = lax.dot_general(
+                docs[these, layer, cols], held[layer, :, cols], (((1,), (1,)), ((), ())),
+                preferred_element_type=jnp.float32,
+            )
+            total = term if total is None else total + term
+        if first_one:
+            acc[these, :] = total
+        else:
+            acc[these, :] += total
+
+    def compute(c):
+        doc_copy(c).wait()
+        for line in range(LINE):
+            arrived(c, line * 2 + (1 - y), True)
+        add(c, 0, n_docs, c == 0)
+
+    stage(0, 0)
+    send(last, me, 2, True)
+    for r in range(n_docs // 128):
+        row = len_ref[pl.ds(r, 1), :].astype(jnp.float32)
+        lengths[pl.ds(r * 128, 128), :] = jnp.broadcast_to(row, (128, 128)).T
+    done = 0
+    for step in range(1, last + LINE):
+        if step < last:
+            take_own(step)
+        if step <= last:
+            stage(step, 0)
+        for hops in range(1, LINE):
+            if 0 <= step - hops <= last:
+                stage(step - hops, hops)
+        if step >= LAG and done < last:
+            compute(done)
+            done += 1
+    while done < last:
+        compute(done)
+        done += 1
+
+    doc_copy(last).wait()
+    blocks = 3
+    height = n_docs // blocks
+
+    def swap(b):
+        these = pl.ds(b * height, height)
+        return pltpu.make_async_remote_copy(
+            src_ref=acc.at[these, pl.ds(pl.multiple_of((1 - core) * half, half), half)],
+            dst_ref=other.at[these, :],
+            send_sem=x_send.at[b],
+            recv_sem=x_recv.at[b],
+            device_id={"layers": 1 - core},
+            device_id_type=pl.DeviceIdType.MESH,
+        )
+
+    for b in range(blocks):
+        add(last, b * height, height, False)
+        swap(b).start()
+    for b in range(blocks):
+        these = pl.ds(b * height, height)
+        swap(b).wait_recv()
+        mine = acc[these, pl.ds(pl.multiple_of(core * half, half), half)]
+        out_ref[these, :] = (mine + other[these, :]) / lengths[these, :]
+    for b in range(blocks):
+        swap(b).wait_send()
+    send(last, me, 2, False)
+    for c in range(last + 1):
+        for hops in range(LINE):
+            stage(c, hops, False)
+
+
+def gathered(n, doc_grads, query_grads, doc_lengths):
+    n_docs, layers, depth = doc_grads.shape
+    rows = query_grads.shape[0]
+    queries = rows * n
+    cuts = pieces_of(depth)
+    count = len(cuts)
+    hbm = pl.BlockSpec(memory_space=pl.ANY)
+    vmem = pl.BlockSpec(memory_space=pltpu.VMEM)
+    return pl.pallas_call(
+        functools.partial(kernel, cuts),
+        out_shape=jax.ShapeDtypeStruct((n_docs, queries // 2), jnp.float32),
+        in_specs=[hbm, hbm, vmem],
+        out_specs=vmem,
+        scratch_shapes=[
+            pltpu.VMEM((n_docs, layers, depth), jnp.bfloat16),
+            pltpu.VMEM((rows, layers, depth), jnp.bfloat16),
+            pltpu.VMEM((layers, queries, depth), jnp.bfloat16),
+            pltpu.VMEM((n_docs, queries), jnp.float32),
+            pltpu.VMEM((n_docs, queries // 2), jnp.float32),
+            pltpu.VMEM((n_docs, 128), jnp.float32),
+            pltpu.SemaphoreType.DMA((count,)),
+            pltpu.SemaphoreType.DMA((count,)),
+            pltpu.SemaphoreType.DMA((3, count, n)),
+            pltpu.SemaphoreType.DMA((count, n)),
+            pltpu.SemaphoreType.DMA((3,)),
+            pltpu.SemaphoreType.DMA((3,)),
+        ],
+        compiler_params=pltpu.CompilerParams(
+            collective_id=0, has_side_effects=True, vmem_limit_bytes=58 * 2**20
+        ),
+        cost_estimate=pl.CostEstimate(
+            flops=2 * n_docs * queries * layers * depth,
+            bytes_accessed=2 * (n_docs + rows) * layers * depth,
+            transcendentals=0,
+        ),
+    )(doc_grads, query_grads, doc_lengths.reshape(n_docs // 128, 128))
+
+
+def plain(doc_grads, query_grads, doc_lengths):
     partial_value = jnp.einsum(
         "dlp,qlp->dq",
         doc_grads,
@@ -16,6 +260,21 @@
 
 
 def solution(mesh):
+    n = mesh.shape["docs"]
+
+    def on_device(doc_grads, query_grads, doc_lengths):
+        fits = (
+            n == 2 * LINE
+            and mesh.shape["layers"] == 2
+            and doc_grads.shape[1] == 2
+            and doc_grads.shape[0] % 384 == 0
+            and doc_grads.shape[2] % 128 == 0
+            and query_grads.shape[0] * n == 256
+        )
+        if fits:
+            return gathered(n, doc_grads, query_grads, doc_lengths)
+        return plain(doc_grads, query_grads, doc_lengths)
+
     in_specs = (
         P(("groups", "docs"), "layers", None),
         P(("groups", "docs"), "layers", None),

time: 115 us -> 64.4 us (0.56)
  waiting for transfers between devices: 83.5 us -> 0 us
  Pallas kernels: 0 us -> 62.4 us
  matrix products: 13.9 us -> 0 us
  between operations: 13.4 us -> 0.01 us
  other arithmetic: 1.92 us -> 0 us
    all_gather x1 -> x0, waiting for transfers between devices: 76.9 us -> none  [on_device(): lax.all_gather(query_grads, 'docs', axis=0, tiled=True)]
    pallas_call x0 -> x1, Pallas kernels: none -> 62.4 us  [gathered(): pl.pallas_call(functools.partial(kernel, cuts), out_shape=jax.ShapeDtypeS...]
    dot_general x1 -> x0, matrix products: 13.9 us -> none  [on_device(): jnp.einsum('dlp,qlp->dq', doc_grads, lax.all_gather(query_grads, 'docs',...]
    reduce_scatter x1 -> x0, waiting for transfers between devices: 6.64 us -> none  [on_device(): lax.psum_scatter(partial_value, 'layers', scatter_dimension=1, tiled=True)]
    div x1 -> x0, other arithmetic: 1.91 us -> none  [on_device(): return summed / doc_lengths.astype(jnp.float32)[:, None]]
  transfers between devices with their start and end apart: 2 -> 0, of which waited for: 2 -> 0; matrix products, arithmetic and copies ran while one was open for 0% -> 0% of each run, Pallas kernels for 0% -> 0%
where the time goes in v1:
time: 64.4 us; the launch traced here: 64.2 us
  Pallas kernels  62.4 us (97%)
  local copies, waits for them, and re-layouts  1.77 us (3%)
    pallas_call x1, Pallas kernels, gathered(): pl.pallas_call(functools.partial(kernel, cuts), out_shape=jax.ShapeDtypeS...  62.4 us
    unnamed x1, local copies, waits for them, and re-layouts  1.77 us

profile of v1, /device:TPU:0, one launch (start us, length us, event | category | flops | bytes accessed | tf_op | source)
XLA Modules:
  0.0 64.2 jit_solution(9170832813422254562)
XLA Ops:
  0.0 62.4 %shard_map.37 = f32[768,128]{1,0:T(8,128)} custom-call(bf16[768,2,4096]{2,1,0:T(2,128)(2,1)} %docs_ref.1, bf16[32,2,4096]{2,1,0:T(2,128)(2,1)} %q_ref.1, s32[6,128]{1,0:T(8,128)} %bitcast.1), custom_call_target="tpu_custom_call" | custom-call | flops 3221225472 | bytes 13107200 | tf_op jit(solution)/shard_map/pallas_call | solution.py:221
  62.4 1.8 %copy.5 = f32[768,128]{1,0:T(8,128)} copy(f32[768,128]{1,0:T(8,128)} %shard_map.37) | data formatting | bytes 786432

commit v2 on v1

--- a/solution.py
+++ b/solution.py
@@ -10,7 +10,7 @@
 LINE = 4
 LAST = 640
 STEP = 512
-LAG = 5
+LAG = 6
 
 
 def pieces_of(depth):
@@ -163,12 +163,14 @@
     for r in range(n_docs // 128):
         row = len_ref[pl.ds(r, 1), :].astype(jnp.float32)
         lengths[pl.ds(r * 128, 128), :] = jnp.broadcast_to(row, (128, 128)).T
+    take_own(1)
+    stage(1, 0)
     done = 0
     for step in range(1, last + LINE):
-        if step < last:
-            take_own(step)
-        if step <= last:
-            stage(step, 0)
+        if step + 1 < last:
+            take_own(step + 1)
+        if step + 1 <= last:
+            stage(step + 1, 0)
         for hops in range(1, LINE):
             if 0 <= step - hops <= last:
                 stage(step - hops, hops)

time: 64.4 us -> 68 us (1.056)
  Pallas kernels: 62.4 us -> 66 us
    pallas_call x1, Pallas kernels: 62.4 us -> 66 us  [gathered(): pl.pallas_call(functools.partial(kernel, cuts), out_shape=jax.ShapeDtypeS...]
where the time goes in v2:
time: 68 us; the launch traced here: 67.8 us
  Pallas kernels  66 us (97%)
  local copies, waits for them, and re-layouts  1.77 us (3%)
    pallas_call x1, Pallas kernels, gathered(): pl.pallas_call(functools.partial(kernel, cuts), out_shape=jax.ShapeDtypeS...  66 us
    unnamed x1, local copies, waits for them, and re-layouts  1.77 us

profile of v2, /device:TPU:0, one launch (start us, length us, event | category | flops | bytes accessed | tf_op | source)
XLA Modules:
  0.0 67.8 jit_solution(3680011202923571264)
XLA Ops:
  0.0 66.0 %shard_map.37 = f32[768,128]{1,0:T(8,128)} custom-call(bf16[768,2,4096]{2,1,0:T(2,128)(2,1)} %docs_ref.1, bf16[32,2,4096]{2,1,0:T(2,128)(2,1)} %q_ref.1, s32[6,128]{1,0:T(8,128)} %bitcast.1), custom_call_target="tpu_custom_call" | custom-call | flops 3221225472 | bytes 13107200 | tf_op jit(solution)/shard_map/pallas_call | solution.py:223
  66.0 1.8 %copy.5 = f32[768,128]{1,0:T(8,128)} copy(f32[768,128]{1,0:T(8,128)} %shard_map.37) | data formatting | bytes 786432
